TPU v7x, 32 devices: a whole 2x2x4 slice. The times are simulated.
32 devices in a mesh: rows: 8 (over z, x), grp: 4 (over y, core).
Axes of the slice: x: 2, y: 2, z: 4, core: 2. Of those that a mesh axis runs over, the one named last changes fastest.
Arguments:
- embeddings: bfloat16 [16384, 1024], P(('rows', 'grp')), may hold values from -6 to 6
- coarse_ids: int32 [16384], P(('rows', 'grp')), may hold values from 0 to 2047, as said below
- fine_ids: int32 [16384], P(('rows', 'grp')), may hold values from 0 to 63, as said below
- coarse_old: float32 [2048, 1024], P(('rows', 'grp')), may hold values from -6 to 6
- fine_old: float32 [2048, 64, 1024], P('rows', 'grp'), may hold values from -6 to 6
Outputs:
- coarse_new: float32 [2048, 1024], P(('rows', 'grp'))
- fine_new: float32 [2048, 64, 1024], P('rows', 'grp')
- distances: float32 [16384], P(('rows', 'grp'))
Inputs may be any that keep to these rules, and one draw needn't show every extreme that they name: Among the 512 rows of one device, at most 32 have the same pair (coarse_ids // 256, fine_ids // 16), and in every such block some pair has exactly 32. `fine_ids`: within each coarse cluster's fine centroids.
All inputs are finite; a program needn't handle non-finite values.
Results may differ from a plain program's by a relative error of at most 0.0003.
Values may be sent and summed in bfloat16 or wider, within the bound.
A program may use at most 128 MiB of HBM per device.

v0:
```python
import jax
import jax.numpy as jnp
from jax import lax
from jax.sharding import PartitionSpec as P


def on_device(embeddings, coarse_ids, fine_ids, coarse_old, fine_old):
    owners = lax.axis_size("rows")
    groups = lax.axis_size("grp")
    dests = owners * groups
    local_rows = embeddings.shape[0]
    width = embeddings.shape[1]
    slot_count = max(2, 2 * local_rows // dests)
    per_owner = fine_old.shape[0]
    per_group = fine_old.shape[1]
    target = coarse_ids // per_owner * groups + fine_ids // per_group
    local_index = coarse_ids % per_owner * per_group + fine_ids % per_group
    dest_table = (target[:, None] == jnp.arange(dests, dtype=jnp.int32)[None, :]).astype(jnp.int32)
    earlier = jnp.cumsum(dest_table, axis=0) - dest_table
    rank_in = jnp.sum(earlier * dest_table, axis=1)
    position = target * slot_count + rank_in
    send_rows = jnp.zeros((dests * slot_count, width), jnp.bfloat16).at[position].set(embeddings)
    send_index = jnp.full((dests * slot_count,), -1, jnp.int32).at[position].set(local_index)
    send_rows = send_rows.reshape(owners, groups, slot_count, width)
    send_index = send_index.reshape(owners, groups, slot_count)
    got_rows, got_index = (
        lax.all_to_all(
            lax.all_to_all(send_rows, "rows", split_axis=0, concat_axis=0, tiled=True),
            "grp",
            split_axis=1,
            concat_axis=1,
            tiled=True,
        ),
        lax.all_to_all(
            lax.all_to_all(send_index, "rows", split_axis=0, concat_axis=0, tiled=True),
            "grp",
            split_axis=1,
            concat_axis=1,
            tiled=True,
        ),
    )
    flat_rows = got_rows.reshape(-1, width)
    flat_index = got_index.reshape(-1)
    centroid_count = per_owner * per_group
    member = jnp.arange(centroid_count, dtype=jnp.int32)[:, None] == flat_index[None, :]
    fine_sums = jnp.dot(member.astype(jnp.bfloat16), flat_rows, preferred_element_type=jnp.float32)
    fine_counts = jnp.sum(member.astype(jnp.float32), axis=1)
    fine_flat = (fine_old.reshape(centroid_count, width) + fine_sums) / (1.0 + fine_counts)[:, None]
    picked = fine_flat[jnp.maximum(flat_index, 0)]
    diff = flat_rows.astype(jnp.float32) - picked
    row_dist = jnp.where(flat_index >= 0, jnp.mean(diff * diff, axis=1), 0.0)
    returned = lax.all_to_all(
        lax.all_to_all(
            row_dist.reshape(owners, groups, slot_count),
            "rows",
            split_axis=0,
            concat_axis=0,
            tiled=True,
        ),
        "grp",
        split_axis=1,
        concat_axis=1,
        tiled=True,
    )
    distances = returned.reshape(-1)[position]
    partial_sums = jnp.sum(fine_sums.reshape(per_owner, per_group, width), axis=1)
    partial_counts = jnp.sum(fine_counts.reshape(per_owner, per_group), axis=1)
    coarse_sums, coarse_counts = (
        lax.psum_scatter(partial_sums, "grp", scatter_dimension=0, tiled=True),
        lax.psum_scatter(partial_counts, "grp", scatter_dimension=0, tiled=True),
    )
    coarse_new = (coarse_old + coarse_sums) / (1.0 + coarse_counts)[:, None]
    return (coarse_new, fine_flat.reshape(fine_old.shape), distances)


def solution(mesh):
    return jax.shard_map(
        on_device,
        mesh=mesh,
        in_specs=(
            P(("rows", "grp"), None),
            P(("rows", "grp")),
            P(("rows", "grp")),
            P(("rows", "grp"), None),
            P("rows", "grp", None),
        ),
        out_specs=(P(("rows", "grp"), None), P("rows", "grp", None), P(("rows", "grp"))),
        check_vma=False,
    )
```

profile of v0, /device:TPU:0, one launch (start us, length us, event | category | flops | bytes accessed | tf_op | source)
XLA Modules:
  0.0 194.7 jit_solution(14409466791415520487)
XLA Ops:
  7.2 0.7 fusion.14
  7.9 1.2 reduce-window.6
  9.4 2.4 %scatter_custom_fusion = s32[1024]{0:T(1024)S(1)} fusion(s32[512]{0:T(512)S(1)} %compare_select_fusion, s32[512]{0:T(512)S(1)} %get-tuple-element.3, s32[]{:T(128)} %constant.59.clone.1), kind=kCustom, calls=%fused_computation.48 | custom fusion | bytes 4100 | tf_op jit(solution)/shard_map/scatter | solution.py:23
  12.0 0.7 reshape.120
  12.7 7.3 %all-to-all-start = ((s32[8,1,128]{2,1,0:T(1,128)}), s32[8,1,128]{2,1,0:T(1,128)S(1)}, u32[]{:S(2)}, u32[]{:S(2)}) async-start(s32[8,1,128]{2,1,0:T(1,128)} %reshape.120), calls=%async_computation | async-start | bytes 8192 | tf_op jit(solution)/shard_map/all_to_all | solution.py:35
  19.9 4.8 %scatter_custom_fusion.1 = bf16[1024,1024]{1,0:T(8,128)(2,1)} fusion(s32[512]{0:T(512)S(1)} %compare_select_fusion, bf16[512,1024]{1,0:T(8,128)(2,1)} %param.5, bf16[]{:T(256)} %constant.70.clone.1), kind=kCustom, calls=%fused_computation.14 | custom fusion | bytes 2097664 | tf_op jit(solution)/shard_map/scatter | solution.py:22
  24.7 1.6 all-to-all-done
  26.3 4.4 %all-to-all-start.2 = ((bf16[8,4,32,1024]{3,2,1,0:T(8,128)(2,1)}), bf16[8,4,32,1024]{3,2,1,0:T(8,128)(2,1)S(1)}, u32[]{:S(2)}, u32[]{:S(2)}) async-start(bf16[8,4,32,1024]{3,2,1,0:T(8,128)(2,1)} %bitcast.44), calls=%async_computation.2 | async-start | bytes 4194304 | tf_op jit(solution)/shard_map/all_to_all | solution.py:28
  31.2 0.7 reduce.3
  32.0 0.7 reshape.122
  32.6 45.7 %all-to-all-done.2 = bf16[8,4,32,1024]{3,2,1,0:T(8,128)(2,1)S(1)} async-done(((bf16[8,4,32,1024]{3,2,1,0:T(8,128)(2,1)}), bf16[8,4,32,1024]{3,2,1,0:T(8,128)(2,1)S(1)}, u32[]{:S(2)}, u32[]{:S(2)}) %all-to-all-start.2) | async-done | bytes 2097184 | tf_op jit(solution)/shard_map/all_to_all | solution.py:28
  78.4 3.2 %all-to-all-start.1 = ((s32[4,1,256]{2,1,0:T(1,128)}), s32[4,1,256]{2,1,0:T(1,128)S(1)}, u32[]{:S(2)}, u32[]{:S(2)}) async-start(s32[4,1,256]{2,1,0:T(1,128)} %reshape.122), calls=%async_computation.1 | async-start | bytes 8192 | tf_op jit(solution)/shard_map/all_to_all | solution.py:34
  81.6 1.5 copy.33
  83.2 2.2 %all-to-all-done.1 = s32[4,1,256]{2,1,0:T(1,128)S(1)} async-done(((s32[4,1,256]{2,1,0:T(1,128)}), s32[4,1,256]{2,1,0:T(1,128)S(1)}, u32[]{:S(2)}, u32[]{:S(2)}) %all-to-all-start.1) | async-done | bytes 4128 | tf_op jit(solution)/shard_map/all_to_all | solution.py:34
  85.4 3.6 %all-to-all-start.3 = ((bf16[8,4,32,1024]{3,2,0,1:T(8,128)(2,1)}), bf16[8,4,32,1024]{3,2,0,1:T(8,128)(2,1)S(1)}, u32[]{:S(2)}, u32[]{:S(2)}) async-start(bf16[8,4,32,1024]{3,2,0,1:T(8,128)(2,1)} %copy.33), calls=%async_computation.3 | async-start | bytes 4194304 | tf_op jit(solution)/shard_map/all_to_all | solution.py:27
  89.2 0.7 reduce.4
  90.2 1.8 convert_reduce_fusion
  92.0 22.7 %all-to-all-done.3 = bf16[8,4,32,1024]{3,2,0,1:T(8,128)(2,1)S(1)} async-done(((bf16[8,4,32,1024]{3,2,0,1:T(8,128)(2,1)}), bf16[8,4,32,1024]{3,2,0,1:T(8,128)(2,1)S(1)}, u32[]{:S(2)}, u32[]{:S(2)}) %all-to-all-start.3) | async-done | bytes 2097184 | tf_op jit(solution)/shard_map/all_to_all | solution.py:27
  114.9 13.8 %bitcast_reduce_fusion = (f32[256,1024]{1,0:T(8,128)}, f32[4096,1024]{1,0:T(8,128)}) fusion(bf16[1024,1024]{1,0:T(8,128)(2,1)S(1)} %bitcast.45, s32[1024]{0:T(1024)S(1)} %eq.49), kind=kOutput, calls=%fused_computation.6 | convolution fusion | flops 8598061056 | bytes 19927040 | tf_op jit(solution)/shard_map/dot_general | solution.py:46
  128.7 17.6 %fusion = f32[4096,1024]{1,0:T(8,128)} fusion(f32[4096,1024]{1,0:T(8,128)} %get-tuple-element.6, f32[256,16,1024]{2,1,0:T(8,128)} %param.9, f32[4096]{0:T(1024)S(1)} %broadcast_add_fusion), kind=kLoop, calls=%fused_computation.5 | loop fusion | flops 8388608 | bytes 50348032 | tf_op jit(solution)/shard_map/div | solution.py:48
  146.3 12.3 %gather_fusion = f32[1024,1024]{1,0:T(8,128)} fusion(f32[4096,1024]{1,0:T(8,128)} %fusion, s32[1024]{0:T(1024)S(1)} %broadcast_clamp_fusion), kind=kCustom, calls=%fused_computation | custom fusion | bytes 8392704 | tf_op jit(solution)/shard_map/gather | solution.py:49
  158.6 2.8 %fusion.4 = f32[8,4,32]{2,0,1:T(8,128)S(1)} fusion(f32[8,4,32,1024]{3,2,1,0:T(8,128)} %bitcast.43, bf16[8,4,32,1024]{3,2,0,1:T(8,128)(2,1)S(1)} %all-to-all-done.3), kind=kLoop, calls=%fused_computation.13 | loop fusion | flops 4193280 | bytes 6295552 | tf_op jit(solution)/shard_map/reduce_sum | solution.py:51
  161.5 0.7 reshape.124
  162.2 3.3 %all-to-all-start.4 = ((f32[8,1,128]{2,1,0:T(1,128)}), f32[8,1,128]{2,1,0:T(1,128)S(1)}, u32[]{:S(2)}, u32[]{:S(2)}) async-start(f32[8,1,128]{2,1,0:T(1,128)} %reshape.124), calls=%async_computation.5 | async-start | bytes 8192 | tf_op jit(solution)/shard_map/all_to_all | solution.py:53
  167.0 6.0 %all-reduce = f32[256]{0:T(256)S(1)} all-reduce(f32[256]{0:T(256)S(1)} %reduce_sum.48), channel_id=3, replica_groups=mesh['rows'=8,'grp'=4] {'grp'}, use_global_device_ids=true, to_apply=%region_9.10.clone | all-reduce | flops 256 | bytes 2048
  173.4 0.7 reduce.5
  174.2 0.7 reshape.126
  174.9 3.2 %all-to-all-start.5 = ((f32[4,1,256]{2,1,0:T(1,128)}), f32[4,1,256]{2,1,0:T(1,128)S(1)}, u32[]{:S(2)}, u32[]{:S(2)}) async-start(f32[4,1,256]{2,1,0:T(1,128)} %reshape.126), calls=%async_computation.6 | async-start | bytes 8192 | tf_op jit(solution)/shard_map/all_to_all | solution.py:52
  178.2 3.7 %all-to-all-done.5 = f32[4,1,256]{2,1,0:T(1,128)S(1)} async-done(((f32[4,1,256]{2,1,0:T(1,128)}), f32[4,1,256]{2,1,0:T(1,128)S(1)}, u32[]{:S(2)}, u32[]{:S(2)}) %all-to-all-start.5) | async-done | bytes 4128 | tf_op jit(solution)/shard_map/all_to_all | solution.py:52
  181.9 0.7 reduce.6
  182.7 3.4 %gather_fusion.1 = f32[512]{0:T(512)} fusion(f32[1024]{0:T(1024)S(1)} %reshape.77, s32[1024]{0:T(1024)S(1)} %pad_clamp_fusion), kind=kCustom, calls=%fused_computation.1 | custom fusion | bytes 6144 | tf_op jit(solution)/shard_map/gather | solution.py:65
  186.1 1.7 add_divide_fusion
  (40 shorter events, 3.4 us)
Async XLA Ops:
  12.7 13.6 %all-to-all-start = ((s32[8,1,128]{2,1,0:T(1,128)}), s32[8,1,128]{2,1,0:T(1,128)S(1)}, u32[]{:S(2)}, u32[]{:S(2)}) async-start(s32[8,1,128]{2,1,0:T(1,128)} %reshape.120), calls=%async_computation | async-start | bytes 8192 | tf_op jit(solution)/shard_map/all_to_all | solution.py:35
  26.3 52.1 %all-to-all-start.2 = ((bf16[8,4,32,1024]{3,2,1,0:T(8,128)(2,1)}), bf16[8,4,32,1024]{3,2,1,0:T(8,128)(2,1)S(1)}, u32[]{:S(2)}, u32[]{:S(2)}) async-start(bf16[8,4,32,1024]{3,2,1,0:T(8,128)(2,1)} %bitcast.44), calls=%async_computation.2 | async-start | bytes 4194304 | tf_op jit(solution)/shard_map/all_to_all | solution.py:28
  78.4 7.0 %all-to-all-start.1 = ((s32[4,1,256]{2,1,0:T(1,128)}), s32[4,1,256]{2,1,0:T(1,128)S(1)}, u32[]{:S(2)}, u32[]{:S(2)}) async-start(s32[4,1,256]{2,1,0:T(1,128)} %reshape.122), calls=%async_computation.1 | async-start | bytes 8192 | tf_op jit(solution)/shard_map/all_to_all | solution.py:34
  85.4 29.3 %all-to-all-start.3 = ((bf16[8,4,32,1024]{3,2,0,1:T(8,128)(2,1)}), bf16[8,4,32,1024]{3,2,0,1:T(8,128)(2,1)S(1)}, u32[]{:S(2)}, u32[]{:S(2)}) async-start(bf16[8,4,32,1024]{3,2,0,1:T(8,128)(2,1)} %copy.33), calls=%async_computation.3 | async-start | bytes 4194304 | tf_op jit(solution)/shard_map/all_to_all | solution.py:27
  89.0 97.1 %reduce-scatter.2.cloned.1.call-start = ((), (), s32[]{:S(2)}) async-start(), calls=%async_computation.7 | async-start | bytes 1310720 | tf_op jit(solution)/shard_map/reduce_scatter | solution.py:69
  158.6 6.9 %copy-start.1 = (u32[32]{0:T(128)S(1)}, u32[32]{0:T(128)}, u32[]{:S(2)}) copy-start(u32[32]{0:T(128)} %constant.76) | copy-start | bytes 388
  158.6 27.5 %copy-start = (f32[64,1024]{1,0:T(8,128)S(1)}, f32[64,1024]{1,0:T(8,128)}, u32[]{:S(2)}) copy-start(f32[64,1024]{1,0:T(8,128)} %param.8) | copy-start | bytes 786436
  162.2 10.8 %all-to-all-start.4 = ((f32[8,1,128]{2,1,0:T(1,128)}), f32[8,1,128]{2,1,0:T(1,128)S(1)}, u32[]{:S(2)}, u32[]{:S(2)}) async-start(f32[8,1,128]{2,1,0:T(1,128)} %reshape.124), calls=%async_computation.5 | async-start | bytes 8192 | tf_op jit(solution)/shard_map/all_to_all | solution.py:53
  174.9 7.0 %all-to-all-start.5 = ((f32[4,1,256]{2,1,0:T(1,128)}), f32[4,1,256]{2,1,0:T(1,128)S(1)}, u32[]{:S(2)}, u32[]{:S(2)}) async-start(f32[4,1,256]{2,1,0:T(1,128)} %reshape.126), calls=%async_computation.6 | async-start | bytes 8192 | tf_op jit(solution)/shard_map/all_to_all | solution.py:52
Sparse Core Ops, SparseCore 0:
  128.8 23.0 reduce-scatter.1
where the time goes:
time: 195 us
  waiting for transfers between devices  75.9 us (39%)
  local copies, waits for them, and re-layouts  30 us (15%)
  other arithmetic  28.9 us (15%)
  starting transfers between devices  25.3 us (13%)
  between operations  14.8 us (8%)
  matrix products  13.8 us (7%)
  blocking collectives  5.96 us (3%)
    all_to_all x1, waiting for transfers between devices, on_device(): lax.all_to_all(send_rows, 'rows', split_axis=0, concat_axis=0, tiled=True)  45.7 us
    all_to_all x1, waiting for transfers between devices, on_device(): lax.all_to_all(lax.all_to_all(send_rows, 'rows', split_axis=0, concat_axi...  22.7 us
    div x1, other arithmetic, on_device(): (fine_old.reshape(centroid_count, width) + fine_sums) / (1.0 + fine_count...  17.6 us
    dot_general x1, matrix products, on_device(): jnp.dot(member.astype(jnp.bfloat16), flat_rows, preferred_element_type=jn...  13.8 us
    gather x1, local copies, waits for them, and re-layouts, on_device(): picked = fine_flat[jnp.maximum(flat_index, 0)]  12.3 us
    all_to_all x1, starting transfers between devices, on_device(): lax.all_to_all(send_index, 'rows', split_axis=0, concat_axis=0, tiled=True)  7.25 us
    unnamed x1, blocking collectives  5.96 us
    scatter x1, local copies, waits for them, and re-layouts, on_device(): jnp.zeros((dests * slot_count, width), jnp.bfloat16).at[position]  4.79 us
  transfers between devices with their start and end apart: 7, of which 5 were waited for; matrix products, arithmetic and copies ran while one was open for 26% of the time, Pallas kernels for 0%

commit v1 on v0

v1 whole, which is shorter than its diff:
```python
import functools

import jax
import jax.numpy as jnp
from jax import lax
from jax.experimental import pallas as pl
from jax.experimental.pallas import tpu as pltpu
from jax.sharding import PartitionSpec as P

MESH = pl.DeviceIdType.MESH
LANES = 128


def greet(owners, groups, own, grp, with_all):
    barrier = pltpu.get_barrier_semaphore()

    def one(k, carry):
        for j in range(groups):
            pl.semaphore_signal(
                barrier,
                inc=1,
                device_id=(lax.rem(own + k, owners), lax.rem(grp + j, groups)),
                device_id_type=MESH,
            )
        return carry

    lax.fori_loop(1, owners, one, 0)
    for j in range(1, groups):
        pl.semaphore_signal(
            barrier, inc=1, device_id=(own, lax.rem(grp + j, groups)), device_id_type=MESH
        )
    pl.semaphore_wait(barrier, owners * groups - 1)


def send_kernel(owners, groups, slots, emb, pos, index, got, got_index, packed, send_sem, recv_sem, isend, irecv, own_sem):
    own, grp = lax.axis_index("rows"), lax.axis_index("grp")
    me = own * groups + grp
    block = groups * slots
    mine = pl.ds(pl.multiple_of(me * slots, slots), slots)
    greet(owners, groups, own, grp, True)

    def pack(owner):
        at = pl.multiple_of(owner * block, block)
        slot = lax.broadcasted_iota(jnp.int32, (block, emb.shape[0]), 0) + at
        hit = jnp.where(slot == pos[...], 1.0, 0.0).astype(jnp.bfloat16)
        packed[pl.ds(at, block), :] = jnp.dot(
            hit, emb[...], preferred_element_type=jnp.float32
        ).astype(jnp.bfloat16)

    def copies(k, j):
        owner, group = lax.rem(own + k, owners), lax.rem(grp + j, groups)
        dest = owner * groups + group
        at = k * groups + j
        rows = pltpu.make_async_remote_copy(
            src_ref=packed.at[pl.ds(pl.multiple_of(dest * slots, slots), slots)],
            dst_ref=got.at[mine],
            send_sem=send_sem.at[at],
            recv_sem=recv_sem.at[at],
            device_id=(owner, group),
            device_id_type=MESH,
        )
        ids = pltpu.make_async_remote_copy(
            src_ref=index.at[dest],
            dst_ref=got_index.at[me],
            send_sem=isend.at[at],
            recv_sem=irecv.at[at],
            device_id=(owner, group),
            device_id_type=MESH,
        )
        return rows, ids

    def step(k, carry):
        pack(lax.rem(own + k, owners))
        for j in range(groups):
            rows, ids = copies(k, j)
            rows.start()
            ids.start()
        return carry

    lax.fori_loop(1, owners, step, 0)
    pack(own)
    for j in range(1, groups):
        rows, ids = copies(0, j)
        rows.start()
        ids.start()
    here = pltpu.make_async_copy(packed.at[mine], got.at[mine], own_sem.at[0])
    here_ids = pltpu.make_async_copy(index.at[me], got_index.at[me], own_sem.at[1])
    here.start()
    here_ids.start()
    here.wait()
    here_ids.wait()
    for j in range(1, groups):
        rows, ids = copies(0, j)
        rows.wait()
        ids.wait()

    def finish(k, carry):
        for j in range(groups):
            rows, ids = copies(k, j)
            rows.wait()
            ids.wait()
        return carry

    lax.fori_loop(1, owners, finish, 0)


def update_kernel(chunk, per_group, idx_s, idx_col, idx_row, rows, old, new, dist, coarse, held, work, in_sem, out_sem):
    count, width = old.shape
    total = rows.shape[0]
    per_owner = coarse.shape[0]
    load = pltpu.make_async_copy(old, held.at[pl.ds(0, count)], in_sem)
    load.start()
    held[count:, :] = jnp.zeros((held.shape[0] - count, width), jnp.float32)
    owner_of = lax.broadcasted_iota(jnp.int32, (per_owner, total), 0)
    low = owner_of * per_group
    ids = idx_row[...]
    part = jnp.where((ids >= low) & (ids < low + per_group) & (ids < count), 1.0, 0.0)
    coarse[:, :width] = jnp.dot(
        part.astype(jnp.bfloat16), rows[...], preferred_element_type=jnp.float32
    )
    coarse[:, width:] = jnp.broadcast_to(
        jnp.sum(part, axis=1, keepdims=True), (per_owner, LANES)
    )
    load.wait()

    def gather(i, carry):
        at = idx_s[i]
        work[pl.ds(i, 1), :] = held[pl.ds(at, 1), :]
        return carry

    lax.fori_loop(0, total, gather, 0, unroll=8)

    def combine(c, carry):
        at = pl.ds(pl.multiple_of(c * chunk, chunk), chunk)
        col = idx_col[at, :]
        same = jnp.where(col == ids, 1.0, 0.0)
        sums = jnp.dot(same.astype(jnp.bfloat16), rows[...], preferred_element_type=jnp.float32)
        number = jnp.sum(same, axis=1, keepdims=True)
        fresh = (work[at, :] + sums) / (1.0 + number)
        diff = rows[at, :].astype(jnp.float32) - fresh
        dist[at, :] = jnp.broadcast_to(
            jnp.sum(diff * diff, axis=1, keepdims=True) / width, (chunk, LANES)
        )
        work[at, :] = fresh
        return carry

    lax.fori_loop(0, total // chunk, combine, 0)

    def scatter(i, carry):
        at = idx_s[i]
        held[pl.ds(at, 1), :] = work[pl.ds(i, 1), :]
        return carry

    lax.fori_loop(0, total, scatter, 0, unroll=8)
    save = pltpu.make_async_copy(held.at[pl.ds(0, count)], new, out_sem)
    save.start()
    save.wait()


def return_kernel(owners, groups, dist, coarse, got_dist, got_coarse, dsend, drecv, csend, crecv, own_sem):
    own, grp = lax.axis_index("rows"), lax.axis_index("grp")
    me = own * groups + grp
    share = coarse.shape[0] // groups
    greet(owners, groups, own, grp, True)

    def sums(j):
        group = lax.rem(grp + j, groups)
        return pltpu.make_async_remote_copy(
            src_ref=coarse.at[pl.ds(pl.multiple_of(group * share, share), share)],
            dst_ref=got_coarse.at[grp],
            send_sem=csend.at[j],
            recv_sem=crecv.at[j],
            device_id=(own, group),
            device_id_type=MESH,
        )

    def back(k, j):
        owner, group = lax.rem(own + k, owners), lax.rem(grp + j, groups)
        return pltpu.make_async_remote_copy(
            src_ref=dist.at[owner * groups + group],
            dst_ref=got_dist.at[me],
            send_sem=dsend.at[k * groups + j],
            recv_sem=drecv.at[k * groups + j],
            device_id=(owner, group),
            device_id_type=MESH,
        )

    for j in range(1, groups):
        sums(j).start()

    def step(k, carry):
        for j in range(groups):
            back(k, j).start()
        return carry

    lax.fori_loop(1, owners, step, 0)
    for j in range(1, groups):
        back(0, j).start()
    here = pltpu.make_async_copy(dist.at[me], got_dist.at[me], own_sem.at[0])
    here_sums = pltpu.make_async_copy(
        coarse.at[pl.ds(pl.multiple_of(grp * share, share), share)], got_coarse.at[grp], own_sem.at[1]
    )
    here.start()
    here_sums.start()
    here.wait()
    here_sums.wait()
    for j in range(1, groups):
        back(0, j).wait()
        sums(j).wait()

    def finish(k, carry):
        for j in range(groups):
            back(k, j).wait()
        return carry

    lax.fori_loop(1, owners, finish, 0)


def on_device(embeddings, coarse_ids, fine_ids, coarse_old, fine_old):
    owners = lax.axis_size("rows")
    groups = lax.axis_size("grp")
    dests = owners * groups
    local_rows, width = embeddings.shape
    slots = max(2, 2 * local_rows // dests)
    slots = (slots + 15) // 16 * 16
    total = dests * slots
    per_owner, per_group = fine_old.shape[:2]
    count = per_owner * per_group
    target = coarse_ids // per_owner * groups + fine_ids // per_group
    local_index = coarse_ids % per_owner * per_group + fine_ids % per_group
    before = jnp.arange(local_rows)[None, :] < jnp.arange(local_rows)[:, None]
    rank = jnp.sum(((target[:, None] == target[None, :]) & before).astype(jnp.int32), axis=1)
    position = target * slots + rank
    slot_ids = jnp.arange(total, dtype=jnp.int32)
    send_index = jnp.min(
        jnp.where(slot_ids[:, None] == position[None, :], local_index[None, :], count), axis=1
    )
    send_index = jnp.pad(send_index.reshape(dests, 1, slots), ((0, 0), (0, 0), (0, LANES - slots)))
    vmem = pl.BlockSpec(memory_space=pltpu.VMEM)
    hbm = pl.BlockSpec(memory_space=pl.ANY)
    sems = pltpu.SemaphoreType.DMA
    got, got_index = pl.pallas_call(
        functools.partial(send_kernel, owners, groups, slots),
        out_shape=(
            jax.ShapeDtypeStruct((total, width), jnp.bfloat16),
            jax.ShapeDtypeStruct((dests, 1, LANES), jnp.int32),
        ),
        in_specs=[vmem, vmem, vmem],
        out_specs=(hbm, vmem),
        scratch_shapes=[
            pltpu.VMEM((total, width), jnp.bfloat16),
            sems((dests,)),
            sems((dests,)),
            sems((dests,)),
            sems((dests,)),
            sems((2,)),
        ],
        compiler_params=pltpu.CompilerParams(
            collective_id=0, has_side_effects=True, vmem_limit_bytes=32 * 2**20
        ),
        name="send_rows",
    )(embeddings, position.reshape(1, local_rows), send_index)
    index = got_index[:, 0, :slots].reshape(total)
    chunk = min(total, 256)
    new, dist, coarse = pl.pallas_call(
        functools.partial(update_kernel, chunk, per_group),
        out_shape=(
            jax.ShapeDtypeStruct((count, width), jnp.float32),
            jax.ShapeDtypeStruct((total, LANES), jnp.float32),
            jax.ShapeDtypeStruct((per_owner, width + LANES), jnp.float32),
        ),
        in_specs=[pl.BlockSpec(memory_space=pltpu.SMEM), vmem, vmem, vmem, hbm],
        out_specs=(hbm, vmem, vmem),
        scratch_shapes=[
            pltpu.VMEM((count + 8, width), jnp.float32),
            pltpu.VMEM((total, width), jnp.float32),
            sems,
            sems,
        ],
        compiler_params=pltpu.CompilerParams(vmem_limit_bytes=56 * 2**20),
        name="update",
    )(index, index.reshape(total, 1), index.reshape(1, total), got, fine_old.reshape(count, width))
    dist_back = jnp.pad(
        dist[:, 0].reshape(dests, 1, slots), ((0, 0), (0, 0), (0, LANES - slots))
    )
    got_dist, got_coarse = pl.pallas_call(
        functools.partial(return_kernel, owners, groups),
        out_shape=(
            jax.ShapeDtypeStruct((dests, 1, LANES), jnp.float32),
            jax.ShapeDtypeStruct((groups, per_owner // groups, width + LANES), jnp.float32),
        ),
        in_specs=[vmem, vmem],
        out_specs=(vmem, vmem),
        scratch_shapes=[
            sems((dests,)),
            sems((dests,)),
            sems((groups,)),
            sems((groups,)),
            sems((2,)),
        ],
        compiler_params=pltpu.CompilerParams(
            collective_id=1, has_side_effects=True, vmem_limit_bytes=32 * 2**20
        ),
        name="send_back",
    )(dist_back, coarse)
    returned = got_dist[:, 0, :slots].reshape(total)
    distances = jnp.sum(
        jnp.where(slot_ids[None, :] == position[:, None], returned[None, :], 0.0), axis=1
    )
    sums = jnp.sum(got_coarse, axis=0)
    coarse_new = (coarse_old + sums[:, :width]) / (1.0 + sums[:, width : width + 1])
    return coarse_new, new.reshape(fine_old.shape), distances


def solution(mesh):
    return jax.shard_map(
        on_device,
        mesh=mesh,
        in_specs=(
            P(("rows", "grp"), None),
            P(("rows", "grp")),
            P(("rows", "grp")),
            P(("rows", "grp"), None),
            P("rows", "grp", None),
        ),
        out_specs=(P(("rows", "grp"), None), P("rows", "grp", None), P(("rows", "grp"))),
        check_vma=False,
    )
```

time: 195 us -> 114 us (0.58)
  Pallas kernels: 0 us -> 102 us
  waiting for transfers between devices: 75.9 us -> 0 us
  other arithmetic: 28.9 us -> 3.24 us
  starting transfers between devices: 25.3 us -> 0 us
  local copies, waits for them, and re-layouts: 30 us -> 8.14 us
  between operations: 14.8 us -> 0.75 us
  matrix products: 13.8 us -> 0 us
  blocking collectives: 5.96 us -> 0 us
    pallas_call x0 -> x3, Pallas kernels: none -> 102 us  [the longest x1 43.4 us: on_device(): pl.pallas_call(functools.partial(send_kernel, owners, groups, slots), out...]
    all_to_all x6 -> x0, waiting for transfers between devices: 75.9 us -> none  [the longest x1 45.7 us: on_device(): lax.all_to_all(send_rows, 'rows', split_axis=0, concat_axis=0, tiled=True)]
    all_to_all x6 -> x0, starting transfers between devices: 25.1 us -> none  [the longest x1 7.25 us: on_device(): lax.all_to_all(send_index, 'rows', split_axis=0, concat_axis=0, tiled=True)]
    div x2 -> x1, other arithmetic: 19.4 us -> 0.8 us  [on_device(): (coarse_old + sums[:, :width]) / (1.0 + sums[:, width:width + 1])]
    gather x2 -> x0, local copies, waits for them, and re-layouts: 15.7 us -> none  [the longest x1 12.3 us: on_device(): picked = fine_flat[jnp.maximum(flat_index, 0)]]
    dot_general x1 -> x0, matrix products: 13.8 us -> none  [on_device(): jnp.dot(member.astype(jnp.bfloat16), flat_rows, preferred_element_type=jn...]
    scatter x2 -> x0, local copies, waits for them, and re-layouts: 7.23 us -> none  [the longest x1 4.79 us: on_device(): jnp.zeros((dests * slot_count, width), jnp.bfloat16).at[position]]
    unnamed x1 -> x0, blocking collectives: 5.96 us -> none
  transfers between devices with their start and end apart: 7 -> 0, of which waited for: 5 -> 0; matrix products, arithmetic and copies ran while one was open for 26% -> 0% of each run, Pallas kernels for 0% -> 0%
where the time goes in v1:
time: 114 us
  Pallas kernels  102 us (89%)
  local copies, waits for them, and re-layouts  8.14 us (7%)
  other arithmetic  3.24 us (3%)
    pallas_call x1, Pallas kernels, on_device(): pl.pallas_call(functools.partial(send_kernel, owners, groups, slots), out...  43.4 us
    pallas_call x1, Pallas kernels, on_device(): pl.pallas_call(functools.partial(return_kernel, owners, groups), out_shap...  31.8 us
    pallas_call x1, Pallas kernels, on_device(): pl.pallas_call(functools.partial(update_kernel, chunk, per_group), out_sh...  26.7 us
    unnamed x8, local copies, waits for them, and re-layouts  3.83 us

profile of v1, /device:TPU:0, one launch (start us, length us, event | category | flops | bytes accessed | tf_op | source)
XLA Modules:
  0.0 114.1 jit_solution(7748503888340323537)
XLA Ops:
  0.6 0.7 fusion.6
  1.3 0.2 convert_reduce_fusion
  1.6 0.4 select_reduce_fusion.1
  2.0 0.1 reshape.25
  2.1 0.0 copy-start.2
  2.1 1.2 %copy-done.2 = bf16[512,1024]{1,0:T(8,128)(2,1)S(1)} copy-done((bf16[512,1024]{1,0:T(8,128)(2,1)S(1)}, bf16[512,1024]{1,0:T(8,128)(2,1)}, u32[]{:S(2)}) %copy-start.2) | copy-done | bytes 1048600
  3.3 43.4 %send_rows.1 = (bf16[1024,1024]{1,0:T(8,128)(2,1)S(1)}, s32[32,1,128]{2,1,0:T(1,128)S(1)}) custom-call(bf16[512,1024]{1,0:T(8,128)(2,1)S(1)} %copy-done.2, s32[1,512]{1,0:T(1,128)S(1)} %bitcast.5, s32[32,1,128]{2,1,0:T(1,128)S(1)} %pad.8.index), custom_call_target="tpu_custom_call" | custom-call | tf_op jit(solution)/shard_map/send_rows/pallas_call | solution.py:242
  46.7 0.0 copy-start
  46.7 1.3 %copy-done = bf16[1024,1024]{1,0:T(8,128)(2,1)} copy-done((bf16[1024,1024]{1,0:T(8,128)(2,1)}, bf16[1024,1024]{1,0:T(8,128)(2,1)S(1)}, u32[]{:S(2)}) %copy-start) | copy-done | bytes 2097176
  48.0 0.1 fusion.9
  48.1 0.7 reshape_reshape_squeeze.7.idx_row
  48.8 0.7 reshape_squeeze.6.idx_s
  49.4 1.3 %reshape_reshape_squeeze.8.idx_col = s32[1024,1]{1,0:T(8,128)} reshape(s32[32,32]{1,0:T(8,128)S(1)} %bitcast.8) | data formatting | bytes 8192 | tf_op jit(solution)/shard_map/reshape;reshape;squeeze | solution.py:282
  50.8 26.7 %update.1 = (f32[4096,1024]{1,0:T(8,128)}, f32[1024,128]{1,0:T(8,128)}, f32[256,1152]{1,0:T(8,128)}) custom-call(s32[1024]{0:T(1024)} %reshape_squeeze.6.idx_s, s32[1024,1]{1,0:T(8,128)} %reshape_reshape_squeeze.8.idx_col, s32[1,1024]{1,0:T(1,128)} %reshape_reshape_squeeze.7.idx_row, bf16[1024,1024]{1,0:T(8,128)(2,1)} %copy-done, f32[4096,1024]{1,0:T(8,128)} %bitcast.6), custom_call_target="tpu_custom_call" | custom-call | tf_op jit(solution)/shard_map/update/pallas_call | solution.py:265
  77.5 0.0 copy-start.3
  77.5 1.3 %slice_reduce_fusion = f32[1024]{0:T(1024)S(1)} fusion(f32[1024,128]{1,0:T(8,128)} %get-tuple-element.12), kind=kLoop, calls=%fused_computation.7 | loop fusion | bytes 8192 | tf_op jit(solution)/shard_map/slice | solution.py:284
  78.8 0.1 reshape_squeeze.7
  78.9 0.0 copy-start.1
  78.9 1.3 %copy-done.1 = f32[256,1152]{1,0:T(8,128)S(1)} copy-done((f32[256,1152]{1,0:T(8,128)S(1)}, f32[256,1152]{1,0:T(8,128)}, u32[]{:S(2)}) %copy-start.1) | copy-done | bytes 1179672
  80.2 31.8 %send_back.1 = (f32[32,1,128]{2,1,0:T(1,128)S(1)}, f32[4,64,1152]{2,1,0:T(8,128)S(1)}) custom-call(f32[32,1,128]{2,1,0:T(1,128)S(1)} %pad.9.dist, f32[256,1152]{1,0:T(8,128)S(1)} %copy-done.1), custom_call_target="tpu_custom_call" | custom-call | tf_op jit(solution)/shard_map/send_back/pallas_call | solution.py:286
  112.0 0.1 reduce_sum.28
  112.1 0.1 fusion.2
  112.2 0.0 copy-done.3
  112.2 0.8 fusion.1
  113.0 0.1 broadcast_in_dim.37
  113.1 0.9 select_reduce_fusion
  (4 shorter events, 0.1 us)
Async XLA Ops:
  2.1 1.2 %copy-start.2 = (bf16[512,1024]{1,0:T(8,128)(2,1)S(1)}, bf16[512,1024]{1,0:T(8,128)(2,1)}, u32[]{:S(2)}) copy-start(bf16[512,1024]{1,0:T(8,128)(2,1)} %emb.1) | copy-start | bytes 3145732
  46.7 1.4 %copy-start = (bf16[1024,1024]{1,0:T(8,128)(2,1)}, bf16[1024,1024]{1,0:T(8,128)(2,1)S(1)}, u32[]{:S(2)}) copy-start(bf16[1024,1024]{1,0:T(8,128)(2,1)S(1)} %get-tuple-element.11.rows) | copy-start | bytes 6291460
  77.5 34.7 %copy-start.3 = (f32[64,1024]{1,0:T(8,128)S(1)}, f32[64,1024]{1,0:T(8,128)}, u32[]{:S(2)}) copy-start(f32[64,1024]{1,0:T(8,128)} %param.8) | copy-start | bytes 786436
  78.9 1.3 %copy-start.1 = (f32[256,1152]{1,0:T(8,128)S(1)}, f32[256,1152]{1,0:T(8,128)}, u32[]{:S(2)}) copy-start(f32[256,1152]{1,0:T(8,128)} %get-tuple-element.13.coarse) | copy-start | bytes 3538948

commit v2 on v1

v2 whole, which is shorter than its diff:
```python
import functools

import jax
import jax.numpy as jnp
from jax import lax
from jax.experimental import pallas as pl
from jax.experimental.pallas import tpu as pltpu
from jax.sharding import PartitionSpec as P

MESH = pl.DeviceIdType.MESH
LANES = 128


def greet(owners, groups, own, grp):
    barrier = pltpu.get_barrier_semaphore()

    def one(k, carry):
        for j in range(groups):
            pl.semaphore_signal(
                barrier,
                inc=1,
                device_id=(lax.rem(own + k, owners), lax.rem(grp + j, groups)),
                device_id_type=MESH,
            )
        return carry

    lax.fori_loop(1, owners, one, 0)
    for j in range(1, groups):
        pl.semaphore_signal(
            barrier, inc=1, device_id=(own, lax.rem(grp + j, groups)), device_id_type=MESH
        )
    pl.semaphore_wait(barrier, owners * groups - 1)


def send_kernel(owners, groups, slots, emb_hbm, old, pos, index, got, got_index, held, packed, send_sem, recv_sem, isend, irecv, own_sem, emb):
    own, grp = lax.axis_index("rows"), lax.axis_index("grp")
    me = own * groups + grp
    block = groups * slots
    mine = pl.ds(pl.multiple_of(me * slots, slots), slots)
    fetch = pltpu.make_async_copy(emb_hbm, emb, own_sem.at[2])
    fetch.start()
    load = pltpu.make_async_copy(old, held, own_sem.at[3])
    load.start()
    greet(owners, groups, own, grp)
    fetch.wait()

    def pack(owner):
        at = pl.multiple_of(owner * block, block)
        slot = lax.broadcasted_iota(jnp.int32, (block, emb.shape[0]), 0) + at
        hit = jnp.where(slot == pos[...], 1.0, 0.0).astype(jnp.bfloat16)
        packed[pl.ds(at, block), :] = jnp.dot(
            hit, emb[...], preferred_element_type=jnp.float32
        ).astype(jnp.bfloat16)

    def copies(k, j):
        owner, group = lax.rem(own + k, owners), lax.rem(grp + j, groups)
        dest = owner * groups + group
        at = k * groups + j
        rows = pltpu.make_async_remote_copy(
            src_ref=packed.at[pl.ds(pl.multiple_of(dest * slots, slots), slots)],
            dst_ref=got.at[mine],
            send_sem=send_sem.at[at],
            recv_sem=recv_sem.at[at],
            device_id=(owner, group),
            device_id_type=MESH,
        )
        ids = pltpu.make_async_remote_copy(
            src_ref=index.at[dest],
            dst_ref=got_index.at[me],
            send_sem=isend.at[at],
            recv_sem=irecv.at[at],
            device_id=(owner, group),
            device_id_type=MESH,
        )
        return rows, ids

    def step(k, carry):
        pack(lax.rem(own + k, owners))
        for j in range(groups):
            rows, ids = copies(k, j)
            rows.start()
            ids.start()
        return carry

    lax.fori_loop(1, owners, step, 0)
    pack(own)
    for j in range(1, groups):
        rows, ids = copies(0, j)
        rows.start()
        ids.start()
    here = pltpu.make_async_copy(packed.at[mine], got.at[mine], own_sem.at[0])
    here_ids = pltpu.make_async_copy(index.at[me], got_index.at[me], own_sem.at[1])
    here.start()
    here_ids.start()
    here.wait()
    here_ids.wait()
    for j in range(1, groups):
        rows, ids = copies(0, j)
        rows.wait()
        ids.wait()

    def finish(k, carry):
        for j in range(groups):
            rows, ids = copies(k, j)
            rows.wait()
            ids.wait()
        return carry

    lax.fori_loop(1, owners, finish, 0)
    load.wait()


def coarse_kernel(slots, groups, per_group, count, index, rows, held, ids_row, ids_col, kept, *parts):
    dests, total = index.shape[0], rows.shape[0]
    share, width = parts[0].shape[0], rows.shape[1]
    ids = jnp.concatenate([index[s][:, :slots] for s in range(dests)], axis=1)
    ids_row[...] = ids
    ids_col[...] = jnp.transpose(jnp.broadcast_to(ids, (LANES, total)))
    grp = lax.axis_index("grp")
    for j, part in enumerate(parts):
        first = lax.rem(grp + j, groups) * share
        low = (lax.broadcasted_iota(jnp.int32, (share, total), 0) + first) * per_group
        hit = jnp.where((ids >= low) & (ids < low + per_group) & (ids < count), 1.0, 0.0)
        part[:, :width] = jnp.dot(
            hit.astype(jnp.bfloat16), rows[...], preferred_element_type=jnp.float32
        )
        part[:, width:] = jnp.broadcast_to(jnp.sum(hit, axis=1, keepdims=True), (share, LANES))


def update_kernel(chunk, slots, index, ids_col, ids_row, rows, held, new, dist, updated, work, out_sem):
    count, width = held.shape
    total = rows.shape[0]
    dests = index.shape[0]
    step = 8
    ids = ids_row[...]

    def each_row(act):
        def source(s, carry):
            def some(i, carry):
                for u in range(step):
                    slot = jnp.minimum(i * step + u, index[s, 0, slots] - 1)
                    act(index[s, 0, slot], s * slots + slot)
                return carry

            return lax.fori_loop(0, (index[s, 0, slots] + step - 1) // step, some, carry)

        lax.fori_loop(0, dests, source, 0)

    def gather(at, row):
        work[pl.ds(row, 1), :] = updated[pl.ds(at, 1), :]

    def scatter(at, row):
        updated[pl.ds(at, 1), :] = work[pl.ds(row, 1), :]

    each_row(gather)

    def combine(c, carry):
        at = pl.ds(pl.multiple_of(c * chunk, chunk), chunk)
        same = jnp.where(ids_col[at, :1] == ids, 1.0, 0.0)
        sums = jnp.dot(same.astype(jnp.bfloat16), rows[...], preferred_element_type=jnp.float32)
        fresh = (work[at, :] + sums) / (1.0 + jnp.sum(same, axis=1, keepdims=True))
        diff = rows[at, :].astype(jnp.float32) - fresh
        work[at, :] = fresh
        far = jnp.broadcast_to(jnp.sum(diff * diff, axis=1, keepdims=True) / width, (chunk, LANES))
        line = jnp.transpose(far)[:1, :]
        for p in range(chunk // slots):
            dist[c * (chunk // slots) + p] = jnp.concatenate(
                [line[:, p * slots : (p + 1) * slots], jnp.zeros((1, LANES - slots), jnp.float32)], axis=1
            )
        return carry

    lax.fori_loop(0, total // chunk, combine, 0)
    each_row(scatter)
    save = pltpu.make_async_copy(updated, new, out_sem)
    save.start()
    save.wait()


def return_kernel(owners, groups, dist, got_dist, dsend, drecv, own_sem):
    own, grp = lax.axis_index("rows"), lax.axis_index("grp")
    me = own * groups + grp
    greet(owners, groups, own, grp)

    def back(k, j):
        owner, group = lax.rem(own + k, owners), lax.rem(grp + j, groups)
        return pltpu.make_async_remote_copy(
            src_ref=dist.at[owner * groups + group],
            dst_ref=got_dist.at[me],
            send_sem=dsend.at[k * groups + j],
            recv_sem=drecv.at[k * groups + j],
            device_id=(owner, group),
            device_id_type=MESH,
        )

    def step(k, carry):
        for j in range(groups):
            back(k, j).start()
        return carry

    lax.fori_loop(1, owners, step, 0)
    for j in range(1, groups):
        back(0, j).start()
    here = pltpu.make_async_copy(dist.at[me], got_dist.at[me], own_sem)
    here.start()
    here.wait()
    for j in range(1, groups):
        back(0, j).wait()

    def finish(k, carry):
        for j in range(groups):
            back(k, j).wait()
        return carry

    lax.fori_loop(1, owners, finish, 0)


def on_device(embeddings, coarse_ids, fine_ids, coarse_old, fine_old):
    owners = lax.axis_size("rows")
    groups = lax.axis_size("grp")
    dests = owners * groups
    local_rows, width = embeddings.shape
    slots = max(2, 2 * local_rows // dests)
    slots = (slots + 15) // 16 * 16
    total = dests * slots
    per_owner, per_group = fine_old.shape[:2]
    count = per_owner * per_group
    target = coarse_ids // per_owner * groups + fine_ids // per_group
    local_index = coarse_ids % per_owner * per_group + fine_ids % per_group
    before = jnp.arange(local_rows)[None, :] < jnp.arange(local_rows)[:, None]
    rank = jnp.sum(((target[:, None] == target[None, :]) & before).astype(jnp.int32), axis=1)
    position = target * slots + rank
    slot_ids = jnp.arange(total, dtype=jnp.int32)
    send_index = jnp.min(
        jnp.where(slot_ids[:, None] == position[None, :], local_index[None, :], count), axis=1
    )
    filled = jnp.sum((target[None, :] == jnp.arange(dests)[:, None]).astype(jnp.int32), axis=1)
    send_index = jnp.concatenate(
        [
            send_index.reshape(dests, 1, slots),
            jnp.broadcast_to(filled[:, None, None], (dests, 1, LANES - slots)),
        ],
        axis=2,
    )
    spare = 8 * 2**20
    vmem = pl.BlockSpec(memory_space=pltpu.VMEM)
    hbm = pl.BlockSpec(memory_space=pl.ANY)
    sems = pltpu.SemaphoreType.DMA
    got, got_index, held = pl.pallas_call(
        functools.partial(send_kernel, owners, groups, slots),
        out_shape=(
            jax.ShapeDtypeStruct((total, width), jnp.bfloat16),
            jax.ShapeDtypeStruct((dests, 1, LANES), jnp.int32),
            jax.ShapeDtypeStruct((count, width), jnp.float32),
        ),
        in_specs=[hbm, hbm, vmem, vmem],
        out_specs=(vmem, vmem, vmem),
        scratch_shapes=[
            pltpu.VMEM((total, width), jnp.bfloat16),
            sems((dests,)),
            sems((dests,)),
            sems((dests,)),
            sems((dests,)),
            sems((4,)),
            pltpu.VMEM((local_rows, width), jnp.bfloat16),
        ],
        compiler_params=pltpu.CompilerParams(
            collective_id=0,
            has_side_effects=True,
            vmem_limit_bytes=total * width * 4 + local_rows * width * 2 + count * width * 4 + spare,
        ),
        cost_estimate=pl.CostEstimate(
            flops=2 * total * local_rows * width,
            bytes_accessed=64 * total * width,
            transcendentals=0,
            remote_bytes_transferred=2 * total * width,
        ),
        name="send_rows",
    )(embeddings, fine_old.reshape(count, width), position.reshape(1, local_rows), send_index)
    share = per_owner // groups
    ids_row, ids_col, held, *parts = pl.pallas_call(
        functools.partial(coarse_kernel, slots, groups, per_group, count),
        out_shape=[
            jax.ShapeDtypeStruct((1, total), jnp.int32),
            jax.ShapeDtypeStruct((total, LANES), jnp.int32),
            jax.ShapeDtypeStruct((count, width), jnp.float32),
        ]
        + [jax.ShapeDtypeStruct((share, width + LANES), jnp.float32)] * groups,
        in_specs=[vmem, vmem, vmem],
        out_specs=[vmem] * (3 + groups),
        input_output_aliases={2: 2},
        compiler_params=pltpu.CompilerParams(
            vmem_limit_bytes=total * width * 2 + per_owner * total * 12 + per_owner * width * 4 + spare
        ),
        name="coarse_part",
    )(got_index, got, held)
    sums = parts[0]
    for j in range(1, groups):
        around = [(g, (g + j) % groups) for g in range(groups)]
        sums = sums + lax.ppermute(parts[j], "grp", around)
    chunk = min(total, 256)
    new, dist, _ = pl.pallas_call(
        functools.partial(update_kernel, chunk, slots),
        out_shape=(
            jax.ShapeDtypeStruct((count, width), jnp.float32),
            jax.ShapeDtypeStruct((dests, 1, LANES), jnp.float32),
            jax.ShapeDtypeStruct((count, width), jnp.float32),
        ),
        in_specs=[pl.BlockSpec(memory_space=pltpu.SMEM), vmem, vmem, vmem, vmem],
        out_specs=(hbm, vmem, vmem),
        input_output_aliases={4: 2},
        scratch_shapes=[
            pltpu.VMEM((total, width), jnp.float32),
            sems,
        ],
        compiler_params=pltpu.CompilerParams(
            vmem_limit_bytes=total * width * 6 + spare
        ),
        cost_estimate=pl.CostEstimate(
            flops=2 * total * total * width, bytes_accessed=8 * count * width, transcendentals=0
        ),
        name="update",
    )(got_index, ids_col, ids_row, got, held)
    got_dist = pl.pallas_call(
        functools.partial(return_kernel, owners, groups),
        out_shape=jax.ShapeDtypeStruct((dests, 1, LANES), jnp.float32),
        in_specs=[vmem],
        out_specs=vmem,
        scratch_shapes=[sems((dests,)), sems((dests,)), sems],
        compiler_params=pltpu.CompilerParams(collective_id=1, has_side_effects=True),
        name="send_back",
    )(dist)
    returned = got_dist[:, 0, :slots].reshape(total)
    distances = jnp.sum(
        jnp.where(slot_ids[None, :] == position[:, None], returned[None, :], 0.0), axis=1
    )
    coarse_new = (coarse_old + sums[:, :width]) / (1.0 + sums[:, width : width + 1])
    return coarse_new, new.reshape(fine_old.shape), distances


def solution(mesh):
    return jax.shard_map(
        on_device,
        mesh=mesh,
        in_specs=(
            P(("rows", "grp"), None),
            P(("rows", "grp")),
            P(("rows", "grp")),
            P(("rows", "grp"), None),
            P("rows", "grp", None),
        ),
        out_specs=(P(("rows", "grp"), None), P("rows", "grp", None), P(("rows", "grp"))),
        check_vma=False,
    )
```

time: 114 us -> 99.6 us (0.87)
  Pallas kernels: 102 us -> 90.5 us
  local copies, waits for them, and re-layouts: 8.14 us -> 2.83 us
  starting transfers between devices: 0 us -> 2.06 us
    pallas_call x1, Pallas kernels: 31.8 us -> 24.1 us  [on_device(): pl.pallas_call(functools.partial(return_kernel, owners, groups), out_shap...]
    pallas_call x1 -> x2, Pallas kernels: 26.7 us -> 22.9 us  [the longest x1 21.1 us: on_device(): pl.pallas_call(functools.partial(update_kernel, chunk, slots), out_shape=...]
    another operation x4 -> x0, local copies, waits for them, and re-layouts: 2.73 us -> none  [the longest x1 1.32 us: on_device(): index.reshape(total, 1)]
    ppermute x0 -> x3, starting transfers between devices: none -> 2.06 us  [on_device(): sums = sums + lax.ppermute(parts[j], 'grp', around)]
    unnamed x8 -> x6, local copies, waits for them, and re-layouts: 3.83 us -> 1.82 us
    slice x2 -> x0, local copies, waits for them, and re-layouts: 1.34 us -> none  [the longest x1 1.29 us: on_device(): dist[:, 0].reshape(dests, 1, slots)]
  transfers between devices with their start and end apart: 0 -> 3, of which waited for: 0 -> 0; matrix products, arithmetic and copies ran while one was open for 0% -> 2% of each run, Pallas kernels for 0% -> 45%
where the time goes in v2:
time: 99.6 us
  Pallas kernels  90.5 us (91%)
  other arithmetic  3.44 us (3%)
  local copies, waits for them, and re-layouts  2.83 us (3%)
  starting transfers between devices  2.06 us (2%)
    pallas_call x1, Pallas kernels, on_device(): pl.pallas_call(functools.partial(send_kernel, owners, groups, slots), out...  43.5 us
    pallas_call x1, Pallas kernels, on_device(): pl.pallas_call(functools.partial(return_kernel, owners, groups), out_shap...  24.1 us
    pallas_call x1, Pallas kernels, on_device(): pl.pallas_call(functools.partial(update_kernel, chunk, slots), out_shape=...  21.1 us
    ppermute x3, starting transfers between devices, on_device(): sums = sums + lax.ppermute(parts[j], 'grp', around)  2.06 us
  transfers between devices with their start and end apart: 3, of which 0 were waited for; matrix products, arithmetic and copies ran while one was open for 2% of the time, Pallas kernels for 45%

profile of v2, /device:TPU:0, one launch (start us, length us, event | category | flops | bytes accessed | tf_op | source)
XLA Modules:
  0.0 99.6 jit_solution(7133075322181085253)
XLA Ops:
  0.6 0.7 fusion.6
  1.3 0.1 convert_reduce_fusion.1
  1.5 0.3 convert_reduce_fusion
  1.7 0.4 select_reduce_fusion.1
  2.1 0.1 reshape.29
  2.2 0.1 broadcast_in_dim.26
  2.3 0.1 pad_add_fusion.index
  2.4 0.0 copy-start
  2.4 1.2 %copy-done = bf16[512,1024]{1,0:T(8,128)(2,1)S(1)} copy-done((bf16[512,1024]{1,0:T(8,128)(2,1)S(1)}, bf16[512,1024]{1,0:T(8,128)(2,1)}, u32[]{:S(2)}) %copy-start) | copy-done | bytes 1048600
  3.6 43.5 %send_rows.1 = (bf16[1024,1024]{1,0:T(8,128)(2,1)S(1)}, s32[32,1,128]{2,1,0:T(1,128)S(1)}, f32[4096,1024]{1,0:T(8,128)S(1)}) custom-call(bf16[512,1024]{1,0:T(8,128)(2,1)S(1)} %copy-done, f32[4096,1024]{1,0:T(8,128)} %bitcast.4, s32[1,512]{1,0:T(1,128)S(1)} %bitcast.3, s32[32,1,128]{2,1,0:T(1,128)S(1)} %pad_add_fusion.index), custom_call_target="tpu_custom_call" | custom-call | flops 1073741824 | bytes 67108864 | tf_op jit(solution)/shard_map/send_rows/pallas_call | solution.py:248
  47.1 1.8 %coarse_part.1 = (s32[1,1024]{1,0:T(1,128)S(1)}, s32[1024,128]{1,0:T(8,128)S(1)}, f32[4096,1024]{1,0:T(8,128)S(1)}, f32[64,1152]{1,0:T(8,128)S(1)}, f32[64,1152]...) custom-call(s32[32,1,128]{2,1,0:T(1,128)S(1)} %get-tuple-element.15.index, ...), custom_call_target="tpu_custom_call", output_to_operand_aliasing={{2}: (2, {})} | custom-call | tf_op jit(solution)/shard_map/coarse_part/pallas_call | solution.py:280
  48.9 0.1 collective-permute-start
  49.0 0.6 collective-permute-start.1
  49.6 1.4 %collective-permute-start.2 = (f32[64,1152]{1,0:T(8,128)S(1)}, f32[64,1152]{1,0:T(8,128)S(1)}, u32[]{:S(2)}, u32[]{:S(2)}) collective-permute-start(f32[64,1152]{1,0:T(8,128)S(1)} %get-tuple-element.21), channel_id=1, source_target_pairs={{0,3},{1,0},{2,1},{3,2},{4,7},{5,4},{6,5},{7,6},{8,11},{9,8},{10,9... | collective-permute-start | bytes 884744 | tf_op jit(solution)/shard_map/ppermute | solution.py:299
  51.0 0.0 copy-start.2
  51.0 21.1 %update.1 = (f32[4096,1024]{1,0:T(8,128)}, f32[32,1,128]{2,1,0:T(1,128)S(1)}, f32[4096,1024]{1,0:T(8,128)S(1)}) custom-call(s32[32,1,128]{2,1,0:T(1,128)S(1)} %get-tuple-element.15.index, s32[1024,128]{1,0:T(8,128)S(1)} %get-tuple-element.22.ids_col, s32[1,1024]{1,0:T(1,128)S(1)} %get-tuple-element.23.ids_row, ...), custom_call_target="tpu_custom_call", output_to_operand_aliasing={{2}: (4, {})} | custom-call | flops 2147483648 | bytes 33554432 | tf_op jit(solution)/shard_map/update/pallas_call | solution.py:301
  72.1 0.0 copy-start.1
  72.1 0.6 copy-done.1
  72.7 24.1 %send_back.1 = f32[32,1,128]{2,1,0:T(1,128)} custom-call(f32[32,1,128]{2,1,0:T(1,128)} %copy-done.1), custom_call_target="tpu_custom_call" | custom-call | tf_op jit(solution)/shard_map/send_back/pallas_call | solution.py:323
  96.9 0.8 slice_reduce_fusion
  97.6 0.1 broadcast_in_dim.46
  97.7 0.9 select_reduce_fusion
  98.6 0.0 collective-permute-done
  98.6 0.0 collective-permute-done.1
  98.6 0.0 collective-permute-done.2
  98.6 0.1 add_add_fusion
  98.7 0.1 fusion.2
  98.8 0.0 copy-done.2
  98.8 0.8 fusion.1
  (1 shorter events, 0.0 us)
Async XLA Ops:
  2.4 1.2 %copy-start = (bf16[512,1024]{1,0:T(8,128)(2,1)S(1)}, bf16[512,1024]{1,0:T(8,128)(2,1)}, u32[]{:S(2)}) copy-start(bf16[512,1024]{1,0:T(8,128)(2,1)} %emb_hbm.1) | copy-start | bytes 3145732
  48.9 49.7 %collective-permute-start = (f32[64,1152]{1,0:T(8,128)S(1)}, f32[64,1152]{1,0:T(8,128)S(1)}, u32[]{:S(2)}, u32[]{:S(2)}) collective-permute-start(f32[64,1152]{1,0:T(8,128)S(1)} %get-tuple-element.19), channel_id=1, source_target_pairs={{0,1},{1,2},{2,3},{3,0},{4,5},{5,6},{6,7},{7,4},{8,9},{9,10},{10,1... | collective-permute-start | bytes 884744 | tf_op jit(solution)/shard_map/ppermute | solution.py:299
  49.0 49.7 %collective-permute-start.1 = (f32[64,1152]{1,0:T(8,128)S(1)}, f32[64,1152]{1,0:T(8,128)S(1)}, u32[]{:S(2)}, u32[]{:S(2)}) collective-permute-start(f32[64,1152]{1,0:T(8,128)S(1)} %get-tuple-element.20), channel_id=1, source_target_pairs={{0,2},{1,3},{2,0},{3,1},{4,6},{5,7},{6,4},{7,5},{8,10},{9,11},{10,... | collective-permute-start | bytes 884744 | tf_op jit(solution)/shard_map/ppermute | solution.py:299
  49.6 49.1 %collective-permute-start.2 = (f32[64,1152]{1,0:T(8,128)S(1)}, f32[64,1152]{1,0:T(8,128)S(1)}, u32[]{:S(2)}, u32[]{:S(2)}) collective-permute-start(f32[64,1152]{1,0:T(8,128)S(1)} %get-tuple-element.21), channel_id=1, source_target_pairs={{0,3},{1,0},{2,1},{3,2},{4,7},{5,4},{6,5},{7,6},{8,11},{9,8},{10,9... | collective-permute-start | bytes 884744 | tf_op jit(solution)/shard_map/ppermute | solution.py:299
  51.0 47.8 %copy-start.2 = (f32[64,1024]{1,0:T(8,128)S(1)}, f32[64,1024]{1,0:T(8,128)}, u32[]{:S(2)}) copy-start(f32[64,1024]{1,0:T(8,128)} %param.8) | copy-start | bytes 786436
  72.1 0.6 copy-start.1

commit v3 on v2

--- a/solution.py
+++ b/solution.py
@@ -44,6 +44,14 @@
     greet(owners, groups, own, grp)
     fetch.wait()
 
+    halves = 2 if owners % 2 == 0 else 1
+    half = owners // halves
+
+    def partner(k):
+        cross = (k + 1) % halves
+        i = lax.rem(own % half + k // halves + 1 - cross, half)
+        return lax.rem(own // half + cross, halves) * half + i
+
     def pack(owner):
         at = pl.multiple_of(owner * block, block)
         slot = lax.broadcasted_iota(jnp.int32, (block, emb.shape[0]), 0) + at
@@ -53,7 +61,7 @@
         ).astype(jnp.bfloat16)
 
     def copies(k, j):
-        owner, group = lax.rem(own + k, owners), lax.rem(grp + j, groups)
+        owner, group = partner(k), lax.rem(grp + j, groups)
         dest = owner * groups + group
         at = k * groups + j
         rows = pltpu.make_async_remote_copy(
@@ -75,17 +83,17 @@
         return rows, ids
 
     def step(k, carry):
-        pack(lax.rem(own + k, owners))
+        pack(partner(k))
         for j in range(groups):
             rows, ids = copies(k, j)
             rows.start()
             ids.start()
         return carry
 
-    lax.fori_loop(1, owners, step, 0)
+    lax.fori_loop(0, owners - 1, step, 0)
     pack(own)
     for j in range(1, groups):
-        rows, ids = copies(0, j)
+        rows, ids = copies(owners - 1, j)
         rows.start()
         ids.start()
     here = pltpu.make_async_copy(packed.at[mine], got.at[mine], own_sem.at[0])
@@ -95,7 +103,7 @@
     here.wait()
     here_ids.wait()
     for j in range(1, groups):
-        rows, ids = copies(0, j)
+        rows, ids = copies(owners - 1, j)
         rows.wait()
         ids.wait()
 
@@ -106,7 +114,7 @@
             ids.wait()
         return carry
 
-    lax.fori_loop(1, owners, finish, 0)
+    lax.fori_loop(0, owners - 1, finish, 0)
     load.wait()
 
 
@@ -252,7 +260,7 @@
             jax.ShapeDtypeStruct((dests, 1, LANES), jnp.int32),
             jax.ShapeDtypeStruct((count, width), jnp.float32),
         ),
-        in_specs=[hbm, hbm, vmem, vmem],
+        in_specs=[pl.BlockSpec(memory_space=pltpu.HBM)] * 2 + [vmem, vmem],
         out_specs=(vmem, vmem, vmem),
         scratch_shapes=[
             pltpu.VMEM((total, width), jnp.bfloat16),
@@ -326,7 +334,9 @@
         in_specs=[vmem],
         out_specs=vmem,
         scratch_shapes=[sems((dests,)), sems((dests,)), sems],
-        compiler_params=pltpu.CompilerParams(collective_id=1, has_side_effects=True),
+        compiler_params=pltpu.CompilerParams(
+            collective_id=1, has_side_effects=True, vmem_limit_bytes=spare
+        ),
         name="send_back",
     )(dist)
     returned = got_dist[:, 0, :slots].reshape(total)

time: 99.6 us -> 95.4 us (0.958)
  Pallas kernels: 90.5 us -> 87.3 us
  local copies, waits for them, and re-layouts: 2.83 us -> 1.52 us
    pallas_call x1, Pallas kernels: 24.1 us -> 8.14 us  [on_device(): pl.pallas_call(functools.partial(return_kernel, owners, groups), out_shap...]
    pallas_call x1, Pallas kernels: 43.5 us -> 55.6 us  [on_device(): pl.pallas_call(functools.partial(send_kernel, owners, groups, slots), out...]
  transfers between devices with their start and end apart: 3 -> 3, of which waited for: 0 -> 0; matrix products, arithmetic and copies ran while one was open for 2% -> 1% of each run, Pallas kernels for 45% -> 31%
where the time goes in v3:
time: 95.4 us; the launch traced here: 95.2 us
  Pallas kernels  87.3 us (92%)
  other arithmetic  3.47 us (4%)
  starting transfers between devices  2.15 us (2%)
  local copies, waits for them, and re-layouts  1.52 us (2%)
    pallas_call x1, Pallas kernels, on_device(): pl.pallas_call(functools.partial(send_kernel, owners, groups, slots), out...  55.6 us
    pallas_call x1, Pallas kernels, on_device(): pl.pallas_call(functools.partial(update_kernel, chunk, slots), out_shape=...  21.8 us
    pallas_call x1, Pallas kernels, on_device(): pl.pallas_call(functools.partial(return_kernel, owners, groups), out_shap...  8.14 us
    ppermute x3, starting transfers between devices, on_device(): sums = sums + lax.ppermute(parts[j], 'grp', around)  2.15 us
  transfers between devices with their start and end apart: 3, of which 0 were waited for; matrix products, arithmetic and copies ran while one was open for 1% of the time, Pallas kernels for 31%

profile of v3, /device:TPU:0, one launch (start us, length us, event | category | flops | bytes accessed | tf_op | source)
XLA Modules:
  0.0 95.2 jit_solution(346306934569743701)
XLA Ops:
  0.6 0.7 fusion.6
  1.3 0.1 convert_reduce_fusion.1
  1.5 0.3 convert_reduce_fusion
  1.7 0.4 select_reduce_fusion.1
  2.1 0.1 reshape.29
  2.2 0.1 broadcast_in_dim.26
  2.3 0.1 pad_add_fusion.index
  2.4 0.0 copy-start
  2.4 1.2 %copy-done = bf16[512,1024]{1,0:T(8,128)(2,1)S(1)} copy-done((bf16[512,1024]{1,0:T(8,128)(2,1)S(1)}, bf16[512,1024]{1,0:T(8,128)(2,1)}, u32[]{:S(2)}) %copy-start) | copy-done | bytes 1048600
  3.6 55.6 %send_rows.1 = (bf16[1024,1024]{1,0:T(8,128)(2,1)S(1)}, s32[32,1,128]{2,1,0:T(1,128)S(1)}, f32[4096,1024]{1,0:T(8,128)S(1)}) custom-call(bf16[512,1024]{1,0:T(8,128)(2,1)S(1)} %copy-done, f32[4096,1024]{1,0:T(8,128)} %bitcast.4, s32[1,512]{1,0:T(1,128)S(1)} %bitcast.3, s32[32,1,128]{2,1,0:T(1,128)S(1)} %pad_add_fusion.index), custom_call_target="tpu_custom_call" | custom-call | flops 1073741824 | bytes 67108864 | tf_op jit(solution)/shard_map/send_rows/pallas_call | solution.py:256
  59.2 1.8 %coarse_part.1 = (s32[1,1024]{1,0:T(1,128)S(1)}, s32[1024,128]{1,0:T(8,128)S(1)}, f32[4096,1024]{1,0:T(8,128)S(1)}, f32[64,1152]{1,0:T(8,128)S(1)}, f32[64,1152]...) custom-call(s32[32,1,128]{2,1,0:T(1,128)S(1)} %get-tuple-element.15.index, ...), custom_call_target="tpu_custom_call", output_to_operand_aliasing={{2}: (2, {})} | custom-call | tf_op jit(solution)/shard_map/coarse_part/pallas_call | solution.py:288
  61.0 0.1 collective-permute-start
  61.1 1.4 %collective-permute-start.1 = (f32[64,1152]{1,0:T(8,128)S(1)}, f32[64,1152]{1,0:T(8,128)S(1)}, u32[]{:S(2)}, u32[]{:S(2)}) collective-permute-start(f32[64,1152]{1,0:T(8,128)S(1)} %get-tuple-element.20), channel_id=1, source_target_pairs={{0,2},{1,3},{2,0},{3,1},{4,6},{5,7},{6,4},{7,5},{8,10},{9,11},{10,... | collective-permute-start | bytes 884744 | tf_op jit(solution)/shard_map/ppermute | solution.py:307
  62.5 0.7 collective-permute-start.2
  63.2 0.0 copy-start.1
  63.2 21.8 %update.1 = (f32[4096,1024]{1,0:T(8,128)}, f32[32,1,128]{2,1,0:T(1,128)S(1)}, f32[4096,1024]{1,0:T(8,128)S(1)}) custom-call(s32[32,1,128]{2,1,0:T(1,128)S(1)} %get-tuple-element.15.index, s32[1024,128]{1,0:T(8,128)S(1)} %get-tuple-element.22.ids_col, s32[1,1024]{1,0:T(1,128)S(1)} %get-tuple-element.23.ids_row, ...), custom_call_target="tpu_custom_call", output_to_operand_aliasing={{2}: (4, {})} | custom-call | flops 2147483648 | bytes 33554432 | tf_op jit(solution)/shard_map/update/pallas_call | solution.py:309
  85.0 8.1 %send_back.1 = f32[32,1,128]{2,1,0:T(1,128)S(1)} custom-call(f32[32,1,128]{2,1,0:T(1,128)S(1)} %get-tuple-element.26.dist), custom_call_target="tpu_custom_call" | custom-call | tf_op jit(solution)/shard_map/send_back/pallas_call | solution.py:331
  93.2 0.1 broadcast_in_dim.46
  93.3 0.9 select_reduce_fusion
  94.2 0.0 collective-permute-done
  94.2 0.0 collective-permute-done.1
  94.2 0.0 collective-permute-done.2
  94.2 0.1 add_add_fusion
  94.3 0.1 fusion.2
  94.4 0.0 copy-done.1
  94.4 0.8 fusion.1
  (2 shorter events, 0.1 us)
Async XLA Ops:
  2.4 1.2 %copy-start = (bf16[512,1024]{1,0:T(8,128)(2,1)S(1)}, bf16[512,1024]{1,0:T(8,128)(2,1)}, u32[]{:S(2)}) copy-start(bf16[512,1024]{1,0:T(8,128)(2,1)} %emb_hbm.1) | copy-start | bytes 3145732
  61.0 33.2 %collective-permute-start = (f32[64,1152]{1,0:T(8,128)S(1)}, f32[64,1152]{1,0:T(8,128)S(1)}, u32[]{:S(2)}, u32[]{:S(2)}) collective-permute-start(f32[64,1152]{1,0:T(8,128)S(1)} %get-tuple-element.19), channel_id=1, source_target_pairs={{0,1},{1,2},{2,3},{3,0},{4,5},{5,6},{6,7},{7,4},{8,9},{9,10},{10,1... | collective-permute-start | bytes 884744 | tf_op jit(solution)/shard_map/ppermute | solution.py:307
  61.1 33.1 %collective-permute-start.1 = (f32[64,1152]{1,0:T(8,128)S(1)}, f32[64,1152]{1,0:T(8,128)S(1)}, u32[]{:S(2)}, u32[]{:S(2)}) collective-permute-start(f32[64,1152]{1,0:T(8,128)S(1)} %get-tuple-element.20), channel_id=1, source_target_pairs={{0,2},{1,3},{2,0},{3,1},{4,6},{5,7},{6,4},{7,5},{8,10},{9,11},{10,... | collective-permute-start | bytes 884744 | tf_op jit(solution)/shard_map/ppermute | solution.py:307
  62.5 31.7 %collective-permute-start.2 = (f32[64,1152]{1,0:T(8,128)S(1)}, f32[64,1152]{1,0:T(8,128)S(1)}, u32[]{:S(2)}, u32[]{:S(2)}) collective-permute-start(f32[64,1152]{1,0:T(8,128)S(1)} %get-tuple-element.21), channel_id=1, source_target_pairs={{0,3},{1,0},{2,1},{3,2},{4,7},{5,4},{6,5},{7,6},{8,11},{9,8},{10,9... | collective-permute-start | bytes 884744 | tf_op jit(solution)/shard_map/ppermute | solution.py:307
  63.2 31.2 %copy-start.1 = (f32[64,1024]{1,0:T(8,128)S(1)}, f32[64,1024]{1,0:T(8,128)}, u32[]{:S(2)}) copy-start(f32[64,1024]{1,0:T(8,128)} %param.8) | copy-start | bytes 786436

commit v4 on v3

--- a/solution.py
+++ b/solution.py
@@ -157,16 +157,14 @@
     def gather(at, row):
         work[pl.ds(row, 1), :] = updated[pl.ds(at, 1), :]
 
-    def scatter(at, row):
-        updated[pl.ds(at, 1), :] = work[pl.ds(row, 1), :]
-
     each_row(gather)
 
     def combine(c, carry):
         at = pl.ds(pl.multiple_of(c * chunk, chunk), chunk)
         same = jnp.where(ids_col[at, :1] == ids, 1.0, 0.0)
         sums = jnp.dot(same.astype(jnp.bfloat16), rows[...], preferred_element_type=jnp.float32)
-        fresh = (work[at, :] + sums) / (1.0 + jnp.sum(same, axis=1, keepdims=True))
+        part = 1.0 / (1.0 + jnp.sum(same, axis=1, keepdims=True))
+        fresh = (work[at, :] + sums) * part
         diff = rows[at, :].astype(jnp.float32) - fresh
         work[at, :] = fresh
         far = jnp.broadcast_to(jnp.sum(diff * diff, axis=1, keepdims=True) / width, (chunk, LANES))
@@ -178,10 +176,18 @@
         return carry
 
     lax.fori_loop(0, total // chunk, combine, 0)
-    each_row(scatter)
-    save = pltpu.make_async_copy(updated, new, out_sem)
-    save.start()
-    save.wait()
+    saves = []
+    for p in range(2):
+        side = pl.ds(p * (width // 2), width // 2)
+
+        def scatter(at, row):
+            updated[pl.ds(at, 1), side] = work[pl.ds(row, 1), side]
+
+        each_row(scatter)
+        saves.append(pltpu.make_async_copy(updated.at[:, side], new.at[:, side], out_sem.at[p]))
+        saves[p].start()
+    for save in saves:
+        save.wait()
 
 
 def return_kernel(owners, groups, dist, got_dist, dsend, drecv, own_sem):
@@ -318,7 +324,7 @@
         input_output_aliases={4: 2},
         scratch_shapes=[
             pltpu.VMEM((total, width), jnp.float32),
-            sems,
+            sems((2,)),
         ],
         compiler_params=pltpu.CompilerParams(
             vmem_limit_bytes=total * width * 6 + spare

time: 95.4 us -> 98.2 us (1.029)
  Pallas kernels: 87.3 us -> 90.7 us
    pallas_call x1, Pallas kernels: 8.14 us -> 10.7 us  [on_device(): pl.pallas_call(functools.partial(return_kernel, owners, groups), out_shap...]
  transfers between devices with their start and end apart: 3 -> 3, of which waited for: 0 -> 0; matrix products, arithmetic and copies ran while one was open for 1% -> 1% of each run, Pallas kernels for 31% -> 34%
where the time goes in v4:
time: 98.2 us; the launch traced here: 98.6 us
  Pallas kernels  90.7 us (92%)
  other arithmetic  3.47 us (4%)
  starting transfers between devices  2.15 us (2%)
  local copies, waits for them, and re-layouts  1.52 us (2%)
    pallas_call x1, Pallas kernels, on_device(): pl.pallas_call(functools.partial(send_kernel, owners, groups, slots), out...  55.6 us
    pallas_call x1, Pallas kernels, on_device(): pl.pallas_call(functools.partial(update_kernel, chunk, slots), out_shape=...  22.6 us
    pallas_call x1, Pallas kernels, on_device(): pl.pallas_call(functools.partial(return_kernel, owners, groups), out_shap...  10.7 us
    ppermute x3, starting transfers between devices, on_device(): sums = sums + lax.ppermute(parts[j], 'grp', around)  2.15 us
  transfers between devices with their start and end apart: 3, of which 0 were waited for; matrix products, arithmetic and copies ran while one was open for 1% of the time, Pallas kernels for 34%

profile of v4, /device:TPU:0, one launch (start us, length us, event | category | flops | bytes accessed | tf_op | source)
XLA Modules:
  0.0 98.6 jit_solution(9745113538257912133)
XLA Ops:
  0.6 0.7 fusion.6
  1.3 0.1 convert_reduce_fusion.1
  1.5 0.3 convert_reduce_fusion
  1.7 0.4 select_reduce_fusion.1
  2.1 0.1 reshape.29
  2.2 0.1 broadcast_in_dim.26
  2.3 0.1 pad_add_fusion.index
  2.4 0.0 copy-start
  2.4 1.2 %copy-done = bf16[512,1024]{1,0:T(8,128)(2,1)S(1)} copy-done((bf16[512,1024]{1,0:T(8,128)(2,1)S(1)}, bf16[512,1024]{1,0:T(8,128)(2,1)}, u32[]{:S(2)}) %copy-start) | copy-done | bytes 1048600
  3.6 55.6 %send_rows.1 = (bf16[1024,1024]{1,0:T(8,128)(2,1)S(1)}, s32[32,1,128]{2,1,0:T(1,128)S(1)}, f32[4096,1024]{1,0:T(8,128)S(1)}) custom-call(bf16[512,1024]{1,0:T(8,128)(2,1)S(1)} %copy-done, f32[4096,1024]{1,0:T(8,128)} %bitcast.4, s32[1,512]{1,0:T(1,128)S(1)} %bitcast.3, s32[32,1,128]{2,1,0:T(1,128)S(1)} %pad_add_fusion.index), custom_call_target="tpu_custom_call" | custom-call | flops 1073741824 | bytes 67108864 | tf_op jit(solution)/shard_map/send_rows/pallas_call | solution.py:262
  59.2 1.8 %coarse_part.1 = (s32[1,1024]{1,0:T(1,128)S(1)}, s32[1024,128]{1,0:T(8,128)S(1)}, f32[4096,1024]{1,0:T(8,128)S(1)}, f32[64,1152]{1,0:T(8,128)S(1)}, f32[64,1152]...) custom-call(s32[32,1,128]{2,1,0:T(1,128)S(1)} %get-tuple-element.15.index, ...), custom_call_target="tpu_custom_call", output_to_operand_aliasing={{2}: (2, {})} | custom-call | tf_op jit(solution)/shard_map/coarse_part/pallas_call | solution.py:294
  61.0 0.1 collective-permute-start
  61.1 1.4 %collective-permute-start.1 = (f32[64,1152]{1,0:T(8,128)S(1)}, f32[64,1152]{1,0:T(8,128)S(1)}, u32[]{:S(2)}, u32[]{:S(2)}) collective-permute-start(f32[64,1152]{1,0:T(8,128)S(1)} %get-tuple-element.20), channel_id=1, source_target_pairs={{0,2},{1,3},{2,0},{3,1},{4,6},{5,7},{6,4},{7,5},{8,10},{9,11},{10,... | collective-permute-start | bytes 884744 | tf_op jit(solution)/shard_map/ppermute | solution.py:313
  62.5 0.7 collective-permute-start.2
  63.2 0.0 copy-start.1
  63.2 22.6 %update.1 = (f32[4096,1024]{1,0:T(8,128)}, f32[32,1,128]{2,1,0:T(1,128)S(1)}, f32[4096,1024]{1,0:T(8,128)S(1)}) custom-call(s32[32,1,128]{2,1,0:T(1,128)S(1)} %get-tuple-element.15.index, s32[1024,128]{1,0:T(8,128)S(1)} %get-tuple-element.22.ids_col, s32[1,1024]{1,0:T(1,128)S(1)} %get-tuple-element.23.ids_row, ...), custom_call_target="tpu_custom_call", output_to_operand_aliasing={{2}: (4, {})} | custom-call | flops 2147483648 | bytes 33554432 | tf_op jit(solution)/shard_map/update/pallas_call | solution.py:315
  85.8 10.7 %send_back.1 = f32[32,1,128]{2,1,0:T(1,128)S(1)} custom-call(f32[32,1,128]{2,1,0:T(1,128)S(1)} %get-tuple-element.26.dist), custom_call_target="tpu_custom_call" | custom-call | tf_op jit(solution)/shard_map/send_back/pallas_call | solution.py:337
  96.6 0.1 broadcast_in_dim.46
  96.6 0.9 select_reduce_fusion
  97.6 0.0 collective-permute-done
  97.6 0.0 collective-permute-done.1
  97.6 0.0 collective-permute-done.2
  97.6 0.1 add_add_fusion
  97.7 0.1 fusion.2
  97.8 0.0 copy-done.1
  97.8 0.8 fusion.1
  (2 shorter events, 0.1 us)
Async XLA Ops:
  2.4 1.2 %copy-start = (bf16[512,1024]{1,0:T(8,128)(2,1)S(1)}, bf16[512,1024]{1,0:T(8,128)(2,1)}, u32[]{:S(2)}) copy-start(bf16[512,1024]{1,0:T(8,128)(2,1)} %emb_hbm.1) | copy-start | bytes 3145732
  61.0 36.6 %collective-permute-start = (f32[64,1152]{1,0:T(8,128)S(1)}, f32[64,1152]{1,0:T(8,128)S(1)}, u32[]{:S(2)}, u32[]{:S(2)}) collective-permute-start(f32[64,1152]{1,0:T(8,128)S(1)} %get-tuple-element.19), channel_id=1, source_target_pairs={{0,1},{1,2},{2,3},{3,0},{4,5},{5,6},{6,7},{7,4},{8,9},{9,10},{10,1... | collective-permute-start | bytes 884744 | tf_op jit(solution)/shard_map/ppermute | solution.py:313
  61.1 36.5 %collective-permute-start.1 = (f32[64,1152]{1,0:T(8,128)S(1)}, f32[64,1152]{1,0:T(8,128)S(1)}, u32[]{:S(2)}, u32[]{:S(2)}) collective-permute-start(f32[64,1152]{1,0:T(8,128)S(1)} %get-tuple-element.20), channel_id=1, source_target_pairs={{0,2},{1,3},{2,0},{3,1},{4,6},{5,7},{6,4},{7,5},{8,10},{9,11},{10,... | collective-permute-start | bytes 884744 | tf_op jit(solution)/shard_map/ppermute | solution.py:313
  62.5 35.1 %collective-permute-start.2 = (f32[64,1152]{1,0:T(8,128)S(1)}, f32[64,1152]{1,0:T(8,128)S(1)}, u32[]{:S(2)}, u32[]{:S(2)}) collective-permute-start(f32[64,1152]{1,0:T(8,128)S(1)} %get-tuple-element.21), channel_id=1, source_target_pairs={{0,3},{1,0},{2,1},{3,2},{4,7},{5,4},{6,5},{7,6},{8,11},{9,8},{10,9... | collective-permute-start | bytes 884744 | tf_op jit(solution)/shard_map/ppermute | solution.py:313
  63.2 34.6 %copy-start.1 = (f32[64,1024]{1,0:T(8,128)S(1)}, f32[64,1024]{1,0:T(8,128)}, u32[]{:S(2)}) copy-start(f32[64,1024]{1,0:T(8,128)} %param.8) | copy-start | bytes 786436
